TPU v7x, 32 devices: a whole 2x2x4 slice. The times are simulated.
32 devices in a mesh: tok: 16 (over z, x, core), head: 2 (over y).
Axes of the slice: x: 2, y: 2, z: 4, core: 2. Of those that a mesh axis runs over, the one named last changes fastest.
Arguments:
- queries: bfloat16 [2, 2, 4096, 8192], P(None, None, 'tok', 'head'), may hold values from -6 to 6
- first_keys: bfloat16 [2, 4096, 8192], P(None, 'tok', 'head'), may hold values from -6 to 6
- first_values: bfloat16 [2, 4096, 8192], P(None, 'tok', 'head'), may hold values from -6 to 6
- first_rates: float32 [2, 16, 4096], P(None, 'head', 'tok'), may hold values from 0.1 to 1
- w_one: bfloat16 [16, 512, 512], P('head'), may hold values from -0.25 to 0.25
- w_three: bfloat16 [16, 512, 512], P('head'), may hold values from -0.25 to 0.25
- w_two: bfloat16 [16, 512, 512], P('head'), may hold values from -0.25 to 0.25
- step_size: float32 [16], P('head'), may hold values from 0.02 to 0.06
- out_gain: float32 [8192], replicated, may hold values from 0.25 to 1.75
Outputs:
- normed_rows: bfloat16 [2, 2, 4096, 8192], P(None, None, ('tok', 'head'))
All inputs are finite; a program needn't handle non-finite values.
Results may differ from a plain program's by a relative error of at most 0.025.
Values may be sent and summed in bfloat16 or wider, within the bound.
A program may use at most 192 MiB of HBM per device.

v0:
```python
import jax
import jax.numpy as jnp
from jax import lax
from jax.sharding import PartitionSpec as P


def shards(
    queries, first_keys, first_values, first_rates, w_one, w_three, w_two, step_size, out_gain
):
    heads_here = w_one.shape[0]
    seq_count = queries.shape[0]
    head_size = w_one.shape[1]

    def split_heads(array):
        return array.reshape(array.shape[:-1] + (heads_here, head_size))

    def apply_fast(inputs, weights):
        split = split_heads(inputs)
        gate_pre = jnp.einsum("tha,hab->thb", split, weights[0], preferred_element_type=jnp.float32)
        up_pre = jnp.einsum("tha,hab->thb", split, weights[1], preferred_element_type=jnp.float32)
        hidden = (gate_pre * jax.nn.sigmoid(gate_pre) * up_pre).astype(jnp.bfloat16)
        result = jnp.einsum("thb,hba->tha", hidden, weights[2], preferred_element_type=jnp.float32)
        return result.astype(jnp.bfloat16).reshape(inputs.shape)

    def renew(weight, total, mean_sq):
        factor = step_size[:, None, None] * lax.rsqrt(mean_sq[:, None, None] + 1e-05)
        return (weight.astype(jnp.float32) - factor * total).astype(jnp.bfloat16)

    def update(weights, partials):
        totals = (
            lax.psum(partials[0].astype(jnp.bfloat16), "tok").astype(jnp.float32),
            lax.psum(partials[1].astype(jnp.bfloat16), "tok").astype(jnp.float32),
            lax.psum(partials[2].astype(jnp.bfloat16), "tok").astype(jnp.float32),
        )
        return tuple(
            (
                renew(weight, total, jnp.mean(total * total, axis=(1, 2)))
                for weight, total in zip(weights, totals)
            )
        )

    def normalize(block):
        values_f = block.astype(jnp.float32)
        mean_sq = jnp.mean(values_f * values_f, axis=-1, keepdims=True)
        return (values_f * lax.rsqrt(mean_sq + 1e-06) * out_gain).astype(jnp.bfloat16)

    def rows_of_group(block):
        return normalize(
            lax.all_to_all(block[None], "head", split_axis=1, concat_axis=2, tiled=True)
        )[0]

    initial = (w_one, w_three, w_two)
    collected = []
    for sequence in range(seq_count):
        first = apply_fast(queries[sequence, 0], initial)
        first = rows_of_group(first)
        split_keys = split_heads(first_keys[sequence])
        gradient_gate_pre = jnp.einsum(
            "tha,hab->thb", split_keys, initial[0], preferred_element_type=jnp.float32
        )
        gradient_up_pre = jnp.einsum(
            "tha,hab->thb", split_keys, initial[1], preferred_element_type=jnp.float32
        )
        sigma = jax.nn.sigmoid(gradient_gate_pre)
        gradient_hidden = (gradient_gate_pre * sigma * gradient_up_pre).astype(jnp.bfloat16)
        scaled = (
            -jnp.transpose(first_rates[sequence])[:, :, None]
            * split_heads(first_values[sequence]).astype(jnp.float32)
        ).astype(jnp.bfloat16)
        back = jnp.einsum("tha,hba->thb", scaled, initial[2], preferred_element_type=jnp.float32)
        d_up = (back * gradient_gate_pre * sigma).astype(jnp.bfloat16)
        d_gate = (
            back * gradient_up_pre * sigma * (1.0 + gradient_gate_pre * (1.0 - sigma))
        ).astype(jnp.bfloat16)
        grad_one = jnp.einsum(
            "tha,thb->hab", split_keys, d_gate, preferred_element_type=jnp.float32
        )
        grad_three = jnp.einsum(
            "tha,thb->hab", split_keys, d_up, preferred_element_type=jnp.float32
        )
        grad_two = jnp.einsum(
            "thb,tha->hba", gradient_hidden, scaled, preferred_element_type=jnp.float32
        )
        partials = (grad_one, grad_three, grad_two)
        renewed = update(initial, partials)
        second = apply_fast(queries[sequence, 1], renewed)
        second = rows_of_group(second)
        collected.append(jnp.stack([first, second]))
    stacked = jnp.stack(collected)
    return stacked


def solution(mesh):
    return jax.shard_map(
        shards,
        mesh=mesh,
        in_specs=(
            P(None, None, "tok", "head"),
            P(None, "tok", "head"),
            P(None, "tok", "head"),
            P(None, "head", "tok"),
            P("head", None, None),
            P("head", None, None),
            P("head", None, None),
            P("head"),
            P(),
        ),
        out_specs=P(None, None, ("tok", "head"), None),
        check_vma=False,
    )
```

profile of v0, /device:TPU:0, one launch (start us, length us, event | category | flops | bytes accessed | tf_op | source)
XLA Modules:
  0.0 753.8 jit_solution(14066923332183202042)
XLA Ops:
  14.6 6.4 fusion.130
  28.0 6.4 fusion.127
  55.0 10.1 %convert_bitcast_fusion.1 = bf16[8,512,512]{1,2,0:T(8,128)(2,1)} fusion(bf16[256,8,512]{0,2,1:T(8,128)(2,1)} %bitcast.328, f32[8,256,512]{1,2,0:T(8,128)} %copy-done.13, f32[8,512,256]{2,1,0:T(8,128)} %fusion.131, f32[8,512,256]{2,1,0:T(8,128)} %fusion.130), kind=kOutput, calls=%fused_computation.119 | convolution fusion | flops 1086324736 | bytes 18874368 | tf_op jit(solution)/shard_map/tha,thb->hab/dot_general | solution.py:75
  65.1 10.1 %convolution_convert_fusion = bf16[8,512,512]{2,1,0:T(8,128)(2,1)} fusion(f32[8,512,256]{2,1,0:T(8,128)} %fusion.131, f32[8,512,256]{2,1,0:T(8,128)} %fusion.130, f32[256,8,512]{2,1,0:T(8,128)S(1)} %bitcast.319, f32[256,8]{0,1:T(8,128)S(1)} %get-tuple-element.24), kind=kOutput, calls=%fused_computation.129 | convolution fusion | flops 1084227584 | bytes 16785408 | tf_op jit(solution)/shard_map/thb,tha->hba/dot_general | solution.py:81
  90.0 9.1 %convert_bitcast_fusion.3 = bf16[8,512,512]{1,2,0:T(8,128)(2,1)} fusion(bf16[256,8,512]{0,2,1:T(8,128)(2,1)S(1)} %bitcast.325, f32[8,256,512]{1,2,0:T(8,128)} %copy-done.14, f32[8,512,256]{2,1,0:T(8,128)} %fusion.128, f32[8,512,256]{2,1,0:T(8,128)} %fusion.127), kind=kOutput, calls=%fused_computation.126 | convolution fusion | flops 1086324736 | bytes 18874368 | tf_op jit(solution)/shard_map/tha,thb->hab/dot_general | solution.py:75
  99.1 10.0 %convolution_convert_fusion.1 = bf16[8,512,512]{2,1,0:T(8,128)(2,1)} fusion(f32[8,512,256]{2,1,0:T(8,128)} %fusion.128, f32[8,512,256]{2,1,0:T(8,128)} %fusion.127, f32[256,8,512]{2,1,0:T(8,128)S(1)} %bitcast.321, f32[256,8]{0,1:T(8,128)S(1)} %get-tuple-element.23), kind=kOutput, calls=%fused_computation.130 | convolution fusion | flops 1084227584 | bytes 16785408 | tf_op jit(solution)/shard_map/thb,tha->hba/dot_general | solution.py:81
  124.2 9.1 %convert_bitcast_fusion.4 = bf16[256,8,512]{2,0,1:T(8,128)(2,1)} fusion(bf16[8,512,512]{2,1,0:T(8,128)(2,1)} %param.15, f32[8,512,256]{2,1,0:T(8,128)} %fusion.129, bf16[8,512,512]{2,1,0:T(8,128)(2,1)} %param.14, bf16[256,8,512]{0,2,1:T(8,128)(2,1)S(1)} %bitcast.339), kind=kOutput, calls=%fused_computation.134 | convolution fusion | flops 2154823680 | bytes 16777216 | tf_op jit(solution)/shard_map/thb,hba->tha/dot_general | solution.py:22
  136.2 7.8 %copy.213 = bf16[1,256,4096]{2,0,1:T(2,128)(2,1)} copy(bf16[1,256,4096]{1,2,0:T(8,128)(2,1)S(1)} %bitcast.342) | data formatting | bytes 4194304 | tf_op jit(solution)/shard_map/broadcast_in_dim;reshape | solution.py:49
  144.5 13.5 %reduce.25 = bf16[256,4096]{1,0:T(8,128)(2,1)S(1)} reduce(bf16[256,1,4096]{2,1,0:T(2,128)(2,1)} %bitcast.332, bf16[]{:T(256)} %broadcast.307), dimensions={1}, to_apply=%bitcast.276.reduce_sub_computation | reduce | bytes 4194306
  164.6 6.5 copy.199
  171.1 6.5 copy.194
  189.9 6.4 fusion.126
  196.4 9.7 %convert_bitcast_fusion.5 = bf16[256,8,512]{2,0,1:T(8,128)(2,1)} fusion(bf16[8,512,512]{2,1,0:T(8,128)(2,1)} %param.15, f32[8,512,256]{2,1,0:T(8,128)} %fusion.126, bf16[8,512,512]{2,1,0:T(8,128)(2,1)} %param.14, bf16[256,8,512]{0,2,1:T(8,128)(2,1)} %bitcast.341), kind=kOutput, calls=%fused_computation.136 | convolution fusion | flops 2154823680 | bytes 16777216 | tf_op jit(solution)/shard_map/thb,hba->tha/dot_general | solution.py:22
  210.0 9.9 %copy.185 = bf16[1,256,4096]{2,0,1:T(2,128)(2,1)} copy(bf16[1,256,4096]{1,2,0:T(8,128)(2,1)} %bitcast.343) | data formatting | bytes 4194304 | tf_op jit(solution)/shard_map/broadcast_in_dim;reshape | solution.py:49
  219.9 14.8 %reduce.24 = bf16[256,4096]{1,0:T(8,128)(2,1)} reduce(bf16[256,1,4096]{2,1,0:T(2,128)(2,1)} %bitcast.334, bf16[]{:T(256)} %broadcast.307), dimensions={1}, to_apply=%bitcast.280.reduce_sub_computation | reduce | bytes 4194306
  246.9 8.1 %copy_convert_fusion = f32[1,256,4096]{2,1,0:T(8,128)} fusion(bf16[1,256,4096]{2,0,1:T(2,128)(2,1)} %bitcast.314), kind=kLoop, calls=%fused_computation.131 | loop fusion | flops 1048576 | bytes 6291456 | tf_op jit(solution)/shard_map/convert_element_type | solution.py:43
  260.7 8.8 %all-to-all-done = bf16[2,2,262144]{2,1,0:T(2,128)(2,1)} async-done(((bf16[2,2,262144]{2,1,0:T(2,128)(2,1)}), bf16[2,2,262144]{2,1,0:T(2,128)(2,1)}, u32[]{:S(2)}, u32[]{:S(2)}) %all-to-all-start) | async-done | bytes 2097184 | tf_op jit(solution)/shard_map/all_to_all | solution.py:49
  273.8 8.0 %copy_convert_fusion.1 = f32[1,256,4096]{2,1,0:T(8,128)} fusion(bf16[1,256,4096]{2,0,1:T(2,128)(2,1)} %bitcast.316), kind=kLoop, calls=%fused_computation.132 | loop fusion | flops 1048576 | bytes 6291456 | tf_op jit(solution)/shard_map/convert_element_type | solution.py:43
  294.5 262.6 %all-reduce.3.cloned.1.call-done = (bf16[8,512,512]{1,2,0:T(8,128)(2,1)}, bf16[8,512,512]{2,1,0:T(8,128)(2,1)}, bf16[8,512,512]{1,2,0:T(8,128)(2,1)}, bf16[8,512...) async-done(((bf16[8,512,512]{1,2,0:T(8,128)(2,1)}, bf16[8,512,512]{2,1,0:T(8,128)(2,1)}, bf16[8,512,512]{1,2,0:T(8,128)(2,1)}, ...) | async-done | bytes 25165840 | tf_op jit(solution)/shard_map/psum | solution.py:32
  573.8 12.9 %fusion.95 = bf16[8,512,256]{2,1,0:T(8,128)(2,1)} fusion(f32[8,512,256]{2,1,0:T(8,128)} %fusion.12, bf16[8,512,512]{2,1,0:T(8,128)(2,1)} %param.15, bf16[8,512,512]{2,1,0:T(8,128)(2,1)} %get-tuple-element.6, f32[8]{0:T(128)S(1)} %get-tuple-element.26, bf16[256,8,512]{0,2,1:T(8,128)(2,1)S(1)} %bitcast.347, bf16[8,512,512]{1,2,0:T(8,128)(2,1)} %copy.194, ...), kind=kOutput, calls=%fused_computation.144 | convolution fusion | flops 2175795200 | bytes 25165888 | tf_op jit(solution)/shard_map/thb,hba->tha/dot_general | solution.py:22
  586.7 9.9 %copy.230 = bf16[1,256,4096]{2,0,1:T(2,128)(2,1)} copy(bf16[1,256,4096]{1,2,0:T(8,128)(2,1)} %bitcast.349) | data formatting | bytes 4194304 | tf_op jit(solution)/shard_map/broadcast_in_dim;reshape | solution.py:49
  596.6 13.4 %reduce.27 = bf16[256,4096]{1,0:T(8,128)(2,1)S(1)} reduce(bf16[256,1,4096]{2,1,0:T(2,128)(2,1)} %bitcast.335, bf16[]{:T(256)} %broadcast.307), dimensions={1}, to_apply=%bitcast.274.reduce_sub_computation | reduce | bytes 4194306
  616.6 7.5 fusion.14
  624.1 13.2 %fusion.90 = bf16[8,512,256]{2,1,0:T(8,128)(2,1)} fusion(f32[8,512,256]{2,1,0:T(8,128)} %fusion.14, bf16[8,512,512]{2,1,0:T(8,128)(2,1)} %param.15, bf16[8,512,512]{2,1,0:T(8,128)(2,1)} %get-tuple-element.9, f32[8]{0:T(128)S(1)} %get-tuple-element.28, bf16[256,8,512]{0,2,1:T(8,128)(2,1)} %bitcast.345, bf16[8,512,512]{1,2,0:T(8,128)(2,1)} %copy.194, ...), kind=kOutput, calls=%fused_computation.143 | convolution fusion | flops 2175795200 | bytes 25165888 | tf_op jit(solution)/shard_map/thb,hba->tha/dot_general | solution.py:22
  637.4 9.9 %copy.204 = bf16[1,256,4096]{2,0,1:T(2,128)(2,1)} copy(bf16[1,256,4096]{1,2,0:T(8,128)(2,1)} %bitcast.348) | data formatting | bytes 4194304 | tf_op jit(solution)/shard_map/broadcast_in_dim;reshape | solution.py:49
  647.2 14.8 %reduce.26 = bf16[256,4096]{1,0:T(8,128)(2,1)} reduce(bf16[256,1,4096]{2,1,0:T(2,128)(2,1)} %bitcast.333, bf16[]{:T(256)} %broadcast.307), dimensions={1}, to_apply=%bitcast.278.reduce_sub_computation | reduce | bytes 4194306
  674.2 10.3 %copy.231 = f32[1,2,128,4096]{2,3,1,0:T(8,128)} copy(bf16[1,2,128,4096]{3,0,2,1:T(2,128)(2,1)} %bitcast.312) | data formatting | bytes 6291456 | tf_op jit(solution)/shard_map/convert_element_type | solution.py:43
  684.5 7.6 %multiply_reduce_fusion = f32[256]{0:T(256)S(1)} fusion(bf16[256,1,4096]{2,1,0:T(2,128)(2,1)} %reshape.393), kind=kLoop, calls=%fused_computation.115 | loop fusion | flops 3145472 | bytes 2098176 | tf_op jit(solution)/shard_map/reduce_sum | solution.py:44
  701.1 7.6 %multiply_reduce_fusion.2 = f32[256]{0:T(256)S(1)} fusion(bf16[256,1,4096]{2,1,0:T(2,128)(2,1)} %reshape.397), kind=kLoop, calls=%fused_computation.122 | loop fusion | flops 3145472 | bytes 2098176 | tf_op jit(solution)/shard_map/reduce_sum | solution.py:44
  708.7 10.3 %copy.205 = f32[1,2,128,4096]{2,3,1,0:T(8,128)} copy(bf16[1,2,128,4096]{3,0,2,1:T(2,128)(2,1)} %bitcast.313) | data formatting | bytes 6291456 | tf_op jit(solution)/shard_map/convert_element_type | solution.py:43
  719.0 6.8 fusion.63
  734.8 11.9 %copy.232 = bf16[2,2,128,8192]{3,2,1,0:T(8,128)(2,1)} copy(bf16[2,2,128,8192]{2,3,1,0:T(8,128)(2,1)} %pad_maximum_fusion) | data formatting | bytes 16777216 | tf_op jit(solution)/shard_map/stack | solution.py:89
  (102 shorter events, 180.1 us)
Async XLA Ops:
  6.5 550.6 %all-reduce.3.cloned.1.call-start = ((), (), s32[]{:S(2)}) async-start(), calls=%async_computation.4 | async-start | bytes 50331648 | tf_op jit(solution)/shard_map/psum | solution.py:32
  14.6 6.4 copy-start.8
  14.6 6.4 copy-start.2
  28.0 6.4 copy-start.5
  28.0 6.4 copy-start.3
  34.4 3.5 copy-start.16
  40.6 3.8 copy-start.20
  40.6 3.8 copy-start
  44.4 5.1 copy-start.9
  47.5 1.9 copy-start.13
  65.1 10.1 %copy-start.12 = (f32[1,256,4096]{2,1,0:T(8,128)S(1)}, f32[1,256,4096]{2,1,0:T(8,128)}, u32[]{:S(2)}) copy-start(f32[1,256,4096]{2,1,0:T(8,128)} %get-tuple-element.15) | copy-start | bytes 12582916
  79.0 5.2 copy-start.6
  82.1 2.0 copy-start.14
  84.1 5.9 copy-start.7
  160.6 77.9 %all-to-all-start.2 = ((bf16[2,2,262144]{2,1,0:T(2,128)(2,1)}), bf16[2,2,262144]{2,1,0:T(2,128)(2,1)S(1)}, u32[]{:S(2)}, u32[]{:S(2)}) async-start(bf16[2,2,262144]{2,1,0:T(2,128)(2,1)} %reshape.394), calls=%async_computation.2 | async-start | bytes 4194304 | tf_op jit(solution)/shard_map/all_to_all | solution.py:49
  238.5 31.0 %all-to-all-start = ((bf16[2,2,262144]{2,1,0:T(2,128)(2,1)}), bf16[2,2,262144]{2,1,0:T(2,128)(2,1)}, u32[]{:S(2)}, u32[]{:S(2)}) async-start(bf16[2,2,262144]{2,1,0:T(2,128)(2,1)} %reshape.398), calls=%async_computation | async-start | bytes 4194304 | tf_op jit(solution)/shard_map/all_to_all | solution.py:49
  287.6 4.6 copy-start.4
  557.1 5.4 copy-start.17
  557.1 9.7 %copy-start.18 = (bf16[8,512,512]{1,2,0:T(8,128)(2,1)S(1)}, bf16[8,512,512]{1,2,0:T(8,128)(2,1)}, u32[]{:S(2)}) copy-start(bf16[8,512,512]{1,2,0:T(8,128)(2,1)} %get-tuple-element.10) | copy-start | bytes 12582916
  562.5 4.3 copy-start.10
  562.5 6.2 copy-start.15
  566.8 1.9 copy-start.21
  566.8 2.2 copy-start.1
  566.8 3.5 copy-start.11
  612.6 53.2 %all-to-all-start.3 = ((bf16[2,2,262144]{2,1,0:T(2,128)(2,1)}), bf16[2,2,262144]{2,1,0:T(2,128)(2,1)S(1)}, u32[]{:S(2)}, u32[]{:S(2)}) async-start(bf16[2,2,262144]{2,1,0:T(2,128)(2,1)} %reshape.392), calls=%async_computation.3 | async-start | bytes 4194304 | tf_op jit(solution)/shard_map/all_to_all | solution.py:49
  665.8 30.8 %all-to-all-start.1 = ((bf16[2,2,262144]{2,1,0:T(2,128)(2,1)}), bf16[2,2,262144]{2,1,0:T(2,128)(2,1)}, u32[]{:S(2)}, u32[]{:S(2)}) async-start(bf16[2,2,262144]{2,1,0:T(2,128)(2,1)} %reshape.396), calls=%async_computation.1 | async-start | bytes 4194304 | tf_op jit(solution)/shard_map/all_to_all | solution.py:49
  708.7 10.3 %copy-start.19 = (f32[8192]{0:T(1024)S(1)}, f32[8192]{0:T(1024)}, u32[]{:S(2)}) copy-start(f32[8192]{0:T(1024)} %param.17) | copy-start | bytes 98308
Sparse Core Ops, SparseCore 0:
  109.2 447.8 all-reduce.2
where the time goes:
time: 761 us; the launch traced here: 754 us
  waiting for transfers between devices  276 us (36%)
  local copies, waits for them, and re-layouts  176 us (23%)
  matrix products  145 us (19%)
  other arithmetic  125 us (16%)
  starting transfers between devices  18.2 us (2%)
  between operations  13.9 us (2%)
    psum x1, waiting for transfers between devices, update(): lax.psum(partials[1].astype(jnp.bfloat16), 'tok').astype(jnp.float32)  263 us
    unnamed x63, local copies, waits for them, and re-layouts  77.4 us
    unnamed x4, other arithmetic  56.4 us
    dot_general x4, matrix products, apply_fast(): jnp.einsum('thb,hba->tha', hidden, weights[2], preferred_element_type=jnp...  44.9 us
    another operation x4, local copies, waits for them, and re-layouts, rows_of_group(): block[None]  37.4 us
    convert_element_type x4, local copies, waits for them, and re-layouts, normalize(): values_f = block.astype(jnp.float32)  32 us
    reduce_sum x8, other arithmetic, normalize(): mean_sq = jnp.mean(values_f * values_f, axis=-1, keepdims=True)  22.1 us
    dot_general x2, matrix products, shards(): jnp.einsum('thb,tha->hba', gradient_hidden, scaled, preferred_element_typ...  20.1 us
  transfers between devices with their start and end apart: 5, of which 3 were waited for; matrix products, arithmetic and copies ran while one was open for 32% of the time, Pallas kernels for 0%

commit v1 on v0

v1 whole, which is shorter than its diff:
```python
import functools

import jax
import jax.numpy as jnp
from jax import lax
from jax.experimental import pallas as pl
from jax.experimental.pallas import tpu as pltpu
from jax.sharding import PartitionSpec as P

MESH = pl.DeviceIdType.MESH
F32 = jnp.float32
BF16 = jnp.bfloat16


def dot(left, right):
    return jnp.dot(left, right, preferred_element_type=F32)


def dot_tn(left, right):
    return lax.dot_general(left, right, (((0,), (0,)), ((), ())), preferred_element_type=F32)


def dot_nt(left, right):
    return lax.dot_general(left, right, (((1,), (1,)), ((), ())), preferred_element_type=F32)


def fast_map(rows, one, three, two):
    gate = dot(rows, one)
    up = dot(rows, three)
    hidden = (gate * jax.nn.sigmoid(gate) * up).astype(BF16)
    return dot(hidden, two).astype(BF16)


def kernel(
    dims,
    queries, keys, scaled, w_one, w_three, w_two, step_size, gain,
    out,
    k_buf, s_buf, q_buf, w_slot, x_slot, own_w, first_buf, second_buf, rows_buf,
    grads, sent, received, renewed,
    slot_sem, own_sem, local_sem, tok_send, tok_recv, first_send, first_recv,
    ex_send, ex_recv, second_send, second_recv, out_sem,
):
    n_tok, n_head, seqs, heads, rows, hd = dims
    members = heads
    steps = (n_tok // members).bit_length() - 1
    sub = rows // n_head
    here = heads * hd
    tok, head = lax.axis_index("tok"), lax.axis_index("head")
    g = lax.rem(tok, members)
    base = tok - g
    rank = lax.div(tok, members)

    def member(j):
        return lax.rem(g + j, members)

    def peer_head(k):
        return lax.rem(head + k, n_head)

    def partner(step):
        bit = 1 << step
        side = lax.rem(lax.div(rank, bit), 2)
        return (rank + bit * (1 - 2 * side)) * members + g

    def cols(index):
        return pl.ds(pl.multiple_of(index * hd, hd), hd)

    def block(index):
        return pl.ds(pl.multiple_of(index * rows, rows), rows)

    barrier = pltpu.get_barrier_semaphore()
    count = 0
    for j in range(members):
        for k in range(n_head):
            if j or k:
                pl.semaphore_signal(
                    barrier, inc=1, device_id=(base + member(j), peer_head(k)), device_id_type=MESH
                )
                count += 1
    for step in range(steps):
        pl.semaphore_signal(
            barrier, inc=1, device_id=(partner(step), head), device_id_type=MESH
        )
        count += 1
    pl.semaphore_wait(barrier, count)

    def token_parts(kind, s, peer):
        source = (keys.at[s], scaled.at[s], queries.at[s, 1])[kind]
        target = (k_buf, s_buf, q_buf)[kind]
        return source.at[:, cols(peer)], target.at[s, block(g), :]

    def token_copy(kind, s, j):
        peer = member(j)
        src, dst = token_parts(kind, s, peer)
        return pltpu.make_async_remote_copy(
            src_ref=src, dst_ref=dst,
            send_sem=tok_send.at[kind, s, j], recv_sem=tok_recv.at[kind, s, j],
            device_id=(base + peer, head), device_id_type=MESH,
        )

    def token_local(kind, s):
        src, dst = token_parts(kind, s, g)
        return pltpu.make_async_copy(src, dst, local_sem.at[kind, s])

    def start_tokens(kinds, s):
        def body(j, carry):
            for kind in kinds:
                token_copy(kind, s, j).start()
            return carry

        lax.fori_loop(1, members, body, 0)
        for kind in kinds:
            token_local(kind, s).start()

    own_copies = [
        pltpu.make_async_copy(w.at[g], own_w.at[i], own_sem.at[i])
        for i, w in enumerate((w_one, w_three, w_two))
    ]
    for s in range(seqs):
        start_tokens((0, 1), s)
    for copy in own_copies:
        copy.start()

    def fetch(h, slot):
        copies = [
            pltpu.make_async_copy(w.at[h], w_slot.at[slot, i], slot_sem.at[slot, i])
            for i, w in enumerate((w_one, w_three, w_two))
        ]
        for s in range(seqs):
            copies.append(
                pltpu.make_async_copy(
                    queries.at[s, 0, :, cols(h)],
                    x_slot.at[slot, pl.ds(s * rows, rows), :],
                    slot_sem.at[slot, 3 + s],
                )
            )
        return copies

    def first_copy(h, s, k):
        dest = peer_head(k)
        return pltpu.make_async_remote_copy(
            src_ref=first_buf.at[h, pl.ds(pl.multiple_of(s * rows + dest * sub, sub), sub), :],
            dst_ref=rows_buf.at[s, 0, :, cols(head * heads + h)],
            send_sem=first_send.at[h, s, k], recv_sem=first_recv.at[h, s, k],
            device_id=(tok, dest), device_id_type=MESH,
        )

    for copy in fetch(0, 0):
        copy.start()

    def first_body(h, carry):
        slot = lax.rem(h, 2)

        @pl.when(h + 1 < heads)
        def _():
            for copy in fetch(h + 1, lax.rem(h + 1, 2)):
                copy.start()

        for copy in fetch(h, slot):
            copy.wait()
        first_buf[h] = fast_map(x_slot[slot], w_slot[slot, 0], w_slot[slot, 1], w_slot[slot, 2])
        for s in range(seqs):
            for k in range(1, n_head):
                first_copy(h, s, k).start()
            rows_buf[s, 0, :, cols(head * heads + h)] = first_buf[
                h, pl.ds(pl.multiple_of(s * rows + head * sub, sub), sub), :
            ]
        return carry

    lax.fori_loop(0, heads, first_body, 0)
    for copy in own_copies:
        copy.wait()

    def add_block(s, b):
        key_rows = k_buf[s, block(b), :]
        scaled_rows = s_buf[s, block(b), :]
        gate = dot(key_rows, own_w[0])
        up = dot(key_rows, own_w[1])
        back = dot_nt(scaled_rows, own_w[2])
        sig = jax.nn.sigmoid(gate)
        swish = gate * sig
        hidden = (swish * up).astype(BF16)
        d_up = (back * swish).astype(BF16)
        d_gate = (back * up * sig * (1.0 + gate * (1.0 - sig))).astype(BF16)
        grads[s, 0] += dot_tn(key_rows, d_gate)
        grads[s, 1] += dot_tn(key_rows, d_up)
        grads[s, 2] += dot_tn(hidden, scaled_rows)

    def exchange(s, step):
        return pltpu.make_async_remote_copy(
            src_ref=sent.at[s, step], dst_ref=received.at[s, step],
            send_sem=ex_send.at[s, step], recv_sem=ex_recv.at[s, step],
            device_id=(partner(step), head), device_id_type=MESH,
        )

    def start_exchange(s, step):
        sent[s, step] = grads[s].astype(BF16)
        exchange(s, step).start()

    for s in range(seqs):
        grads[s] = jnp.zeros_like(grads[s])
        for kind in (0, 1):
            token_local(kind, s).wait()
        add_block(s, g)

        def grad_body(j, carry):
            for kind in (0, 1):
                token_copy(kind, s, j).wait_recv()
            add_block(s, lax.rem(g + members - j, members))
            return carry

        lax.fori_loop(1, members, grad_body, 0)
        if steps:
            start_exchange(s, 0)
        start_tokens((2,), s)

    tile = 16

    def normalize(s, group):
        def body(r, carry):
            at = pl.ds(pl.multiple_of(r * tile, tile), tile)
            values = rows_buf[s, group, at, :].astype(F32)
            mean_sq = jnp.mean(values * values, axis=-1, keepdims=True)
            rows_buf[s, group, at, :] = (
                values * lax.rsqrt(mean_sq + 1e-06) * gain[...]
            ).astype(BF16)
            return carry

        lax.fori_loop(0, sub // tile, body, 0)
        out_copy(s, group).start()

    def out_copy(s, group):
        return pltpu.make_async_copy(
            rows_buf.at[s, group], out.at[s, group], out_sem.at[s, group]
        )

    def wait_first(h, carry):
        for s in range(seqs):
            for k in range(1, n_head):
                first_copy(h, s, k).wait()
        return carry

    lax.fori_loop(0, heads, wait_first, 0)
    for s in range(seqs):
        normalize(s, 0)

    def second_copy(s, j, k):
        b, dest = member(j), peer_head(k)
        return pltpu.make_async_remote_copy(
            src_ref=second_buf.at[
                s, pl.ds(pl.multiple_of(b * rows + dest * sub, sub), sub), :
            ],
            dst_ref=rows_buf.at[s, 1, :, cols(head * heads + g)],
            send_sem=second_send.at[s, j, k], recv_sem=second_recv.at[s, j, k],
            device_id=(base + b, dest), device_id_type=MESH,
        )

    rate = step_size[g]
    for s in range(seqs):
        for step in range(steps):
            exchange(s, step).wait()
            grads[s] += received[s, step].astype(F32)
            if step + 1 < steps:
                start_exchange(s, step + 1)
        for i in range(3):
            total = grads[s, i]
            mean_sq = jnp.mean(
                jnp.mean(total * total, axis=0, keepdims=True), axis=1, keepdims=True
            )
            renewed[i] = (
                own_w[i].astype(F32) - rate * total * lax.rsqrt(mean_sq + 1e-05)
            ).astype(BF16)

        def wait_queries(j, carry):
            token_copy(2, s, j).wait_recv()
            return carry

        lax.fori_loop(1, members, wait_queries, 0)
        token_local(2, s).wait()

        def second_block(b):
            second_buf[s, block(b), :] = fast_map(
                q_buf[s, block(b), :], renewed[0], renewed[1], renewed[2]
            )

        def second_body(j, carry):
            second_block(member(j))
            for k in range(n_head):
                second_copy(s, j, k).start()
            return carry

        lax.fori_loop(1, members, second_body, 0)
        second_block(g)
        for k in range(1, n_head):
            second_copy(s, 0, k).start()
        rows_buf[s, 1, :, cols(head * heads + g)] = second_buf[
            s, pl.ds(pl.multiple_of(g * rows + head * sub, sub), sub), :
        ]

    for s in range(seqs):
        for k in range(1, n_head):
            second_copy(s, 0, k).wait()

        def wait_second(j, carry):
            for k in range(n_head):
                second_copy(s, j, k).wait()
            return carry

        lax.fori_loop(1, members, wait_second, 0)
        normalize(s, 1)

    def drain(j, carry):
        for s in range(seqs):
            for kind in range(3):
                token_copy(kind, s, j).wait_send()
        return carry

    lax.fori_loop(1, members, drain, 0)
    for s in range(seqs):
        for group in range(2):
            out_copy(s, group).wait()


def solution(mesh):
    n_tok, n_head = mesh.shape["tok"], mesh.shape["head"]

    def shards(
        queries, first_keys, first_values, first_rates, w_one, w_three, w_two, step_size, out_gain
    ):
        seqs, groups, rows, here = queries.shape
        heads, hd, hh = w_one.shape
        members = heads
        steps = (n_tok // members).bit_length() - 1
        sub = rows // n_head
        width = here * n_head
        values = first_values.reshape(seqs, rows, heads, hd).astype(F32)
        rates = jnp.transpose(first_rates, (0, 2, 1))[..., None]
        scaled = (-rates * values).astype(BF16).reshape(first_values.shape)
        anywhere = pl.BlockSpec(memory_space=pl.ANY)
        vmem = pl.BlockSpec(memory_space=pltpu.VMEM)
        smem = pl.BlockSpec(memory_space=pltpu.SMEM)
        sem = pltpu.SemaphoreType.DMA
        dims = (n_tok, n_head, seqs, heads, rows, hd)
        group_rows = members * rows
        flops = 24 * seqs * heads * rows * hd * hh
        return pl.pallas_call(
            functools.partial(kernel, dims),
            out_shape=jax.ShapeDtypeStruct((seqs, groups, sub, width), BF16),
            in_specs=[anywhere] * 6 + [smem, vmem],
            out_specs=anywhere,
            scratch_shapes=[
                pltpu.VMEM((seqs, group_rows, hd), BF16),
                pltpu.VMEM((seqs, group_rows, hd), BF16),
                pltpu.VMEM((seqs, group_rows, hd), BF16),
                pltpu.VMEM((2, 3, hd, hh), BF16),
                pltpu.VMEM((2, seqs * rows, hd), BF16),
                pltpu.VMEM((3, hd, hh), BF16),
                pltpu.VMEM((heads, seqs * rows, hd), BF16),
                pltpu.VMEM((seqs, group_rows, hd), BF16),
                pltpu.VMEM((seqs, groups, sub, width), BF16),
                pltpu.VMEM((seqs, 3, hd, hh), F32),
                pltpu.VMEM((seqs, max(steps, 1), 3, hd, hh), BF16),
                pltpu.VMEM((seqs, max(steps, 1), 3, hd, hh), BF16),
                pltpu.VMEM((3, hd, hh), BF16),
                sem((2, 3 + seqs)),
                sem((3,)),
                sem((3, seqs)),
                sem((3, seqs, members)),
                sem((3, seqs, members)),
                sem((heads, seqs, n_head)),
                sem((heads, seqs, n_head)),
                sem((seqs, max(steps, 1))),
                sem((seqs, max(steps, 1))),
                sem((seqs, members, n_head)),
                sem((seqs, members, n_head)),
                sem((seqs, groups)),
            ],
            compiler_params=pltpu.CompilerParams(
                collective_id=0, has_side_effects=True, vmem_limit_bytes=60 * 1024 * 1024
            ),
            cost_estimate=pl.CostEstimate(
                flops=flops, bytes_accessed=queries.size * 8, transcendentals=0
            ),
        )(queries, first_keys, scaled, w_one, w_three, w_two, step_size, out_gain[None, :])

    return jax.shard_map(
        shards,
        mesh=mesh,
        in_specs=(
            P(None, None, "tok", "head"),
            P(None, "tok", "head"),
            P(None, "tok", "head"),
            P(None, "head", "tok"),
            P("head", None, None),
            P("head", None, None),
            P("head", None, None),
            P("head"),
            P(),
        ),
        out_specs=P(None, None, ("tok", "head"), None),
        check_vma=False,
    )
```

time: 761 us -> 293 us (0.39)
  waiting for transfers between devices: 276 us -> 0 us
  Pallas kernels: 0 us -> 262 us
  local copies, waits for them, and re-layouts: 176 us -> 21 us
  matrix products: 145 us -> 0 us
  other arithmetic: 125 us -> 8.72 us
  starting transfers between devices: 18.2 us -> 0 us
  between operations: 13.9 us -> 0.02 us
    psum x1 -> x0, waiting for transfers between devices: 263 us -> none  [update(): lax.psum(partials[1].astype(jnp.bfloat16), 'tok').astype(jnp.float32)]
    pallas_call x0 -> x1, Pallas kernels: none -> 262 us  [shards(): pl.pallas_call(functools.partial(kernel, dims), out_shape=jax.ShapeDtypeS...]
    dot_general x20 -> x0, matrix products: 145 us -> none  [the longest x4 44.9 us: apply_fast(): jnp.einsum('thb,hba->tha', hidden, weights[2], preferred_element_type=jnp...]
    unnamed x63 -> x1, local copies, waits for them, and re-layouts: 77.4 us -> 7.77 us
    unnamed x4 -> x0, other arithmetic: 56.4 us -> none
    another operation x5 -> x0, local copies, waits for them, and re-layouts: 49.4 us -> none  [the longest x4 37.4 us: rows_of_group(): block[None]]
    convert_element_type x6 -> x0, local copies, waits for them, and re-layouts: 38.8 us -> none  [the longest x4 32 us: normalize(): values_f = block.astype(jnp.float32)]
    reduce_sum x11 -> x0, other arithmetic: 33.7 us -> none  [the longest x8 22.1 us: normalize(): mean_sq = jnp.mean(values_f * values_f, axis=-1, keepdims=True)]
  transfers between devices with their start and end apart: 5 -> 0, of which waited for: 3 -> 0; matrix products, arithmetic and copies ran while one was open for 32% -> 0% of each run, Pallas kernels for 0% -> 0%
where the time goes in v1:
time: 293 us; the launch traced here: 292 us
  Pallas kernels  262 us (89%)
  local copies, waits for them, and re-layouts  21 us (7%)
  other arithmetic  8.72 us (3%)
    pallas_call x1, Pallas kernels, shards(): pl.pallas_call(functools.partial(kernel, dims), out_shape=jax.ShapeDtypeS...  262 us
    mul x2, local copies, waits for them, and re-layouts, shards(): scaled = (-rates * values).astype(BF16).reshape(first_values.shape)  13.1 us
    convert_element_type x1, other arithmetic, shards(): scaled = (-rates * values).astype(BF16).reshape(first_values.shape)  8 us
    unnamed x1, local copies, waits for them, and re-layouts  7.77 us

profile of v1, /device:TPU:0, one launch (start us, length us, event | category | flops | bytes accessed | tf_op | source)
XLA Modules:
  0.0 291.6 jit_solution(3458112673268925276)
XLA Ops:
  0.0 0.7 negate_bitcast_fusion
  0.7 0.1 copy.10
  0.9 3.8 %mul.11 = f32[2,256,8,512]{3,2,1,0:T(8,128)} broadcast(f32[2,256,8]{2,1,0:T(8,128)S(1)} %copy.10), dimensions={0,1,2} | broadcast | bytes 8404992 | tf_op jit(solution)/shard_map/mul | solution.py:337
  4.6 9.4 %mul.12 = f32[2,256,4096]{2,1,0:T(8,128)} reshape(f32[2,256,8,512]{3,2,1,0:T(8,128)} %mul.11) | data formatting | bytes 16777216 | tf_op jit(solution)/shard_map/mul | solution.py:337
  14.0 8.0 %multiply_convert_fusion.scaled = bf16[2,256,4096]{2,1,0:T(8,128)(2,1)} fusion(f32[2,256,4096]{2,1,0:T(8,128)} %mul.12, bf16[2,256,4096]{2,1,0:T(8,128)(2,1)} %param.11), kind=kLoop, calls=%fused_computation | loop fusion | flops 6291456 | bytes 16777216 | tf_op jit(solution)/shard_map/convert_element_type | solution.py:337
  22.0 261.9 %shard_map.91 = bf16[2,2,128,8192]{3,2,1,0:T(8,128)(2,1)} custom-call(bf16[2,2,256,4096]{3,2,1,0:T(8,128)(2,1)} %queries.1, bf16[2,256,4096]{2,1,0:T(8,128)(2,1)} %keys.1, bf16[2,256,4096]{2,1,0:T(8,128)(2,1)} %multiply_convert_fusion.scaled, bf16[8,512,512]{2,1,0:T(8,128)(2,1)} %w_one.1, bf16[8,512,512]{2,1,0:T(8,128)(2,1)} %w_three.1, ...), custom_call_target="tpu_custom_call" | custom-call | flops 25769803776 | bytes 33554432 | tf_op jit(solution)/shard_map/pallas_call | solution.py:345
  283.9 7.8 %copy.12 = bf16[2,2,128,8192]{3,2,1,0:T(8,128)(2,1)} copy(bf16[2,2,128,8192]{3,2,1,0:T(8,128)(2,1)} %shard_map.91) | data formatting | bytes 16777216

commit v2 on v1

v2 whole, which is shorter than its diff:
```python
import functools
import math

import jax
import jax.numpy as jnp
from jax import lax
from jax.experimental import pallas as pl
from jax.experimental.pallas import tpu as pltpu
from jax.sharding import PartitionSpec as P

MESH = pl.DeviceIdType.MESH
F32 = jnp.float32
BF16 = jnp.bfloat16


def dot(left, right):
    return jnp.dot(left, right, preferred_element_type=F32)


def dot_tn(left, right):
    return lax.dot_general(left, right, (((0,), (0,)), ((), ())), preferred_element_type=F32)


def dot_nt(left, right):
    return lax.dot_general(left, right, (((1,), (1,)), ((), ())), preferred_element_type=F32)


def fast_map(rows, one, three, two):
    gate = dot(rows, one)
    up = dot(rows, three)
    hidden = (gate * jax.nn.sigmoid(gate) * up).astype(BF16)
    return dot(hidden, two).astype(BF16)


def kernel(
    dims,
    queries, keys, values, w_one, w_three, w_two, step_size, rates,
    out,
    k_buf, s_buf, q_buf, v_buf, w_slot, x_slot, own_w, first_buf,
    acc, own, from_left, from_right, renewed,
    slot_sem, own_sem, v_sem, local_sem, tok_send, tok_recv, first_send, first_recv, first_local,
    right_send, right_recv, left_send, left_recv, second_send, second_recv, second_local,
):
    n_tok, n_head, seqs, heads, rows, hd, members = dims
    each = heads // members
    chunks = seqs * each
    units = 3 * chunks
    ranks = n_tok // members
    sub = rows // n_head
    tok, head = lax.axis_index("tok"), lax.axis_index("head")
    g = lax.rem(tok, members)
    base = tok - g
    rank = lax.div(tok, members)
    right = lax.rem(tok + members, n_tok)
    left = lax.rem(tok + n_tok - members, n_tok)

    def member(j):
        return lax.rem(g + j, members)

    def peer_head(k):
        return lax.rem(head + k, n_head)

    def cols(index):
        return pl.ds(pl.multiple_of(index * hd, hd), hd)

    def block(index):
        return pl.ds(pl.multiple_of(index * rows, rows), rows)

    barrier = pltpu.get_barrier_semaphore()
    count = 0
    for j in range(members):
        for k in range(n_head):
            if j or k:
                pl.semaphore_signal(
                    barrier, inc=1, device_id=(base + member(j), peer_head(k)), device_id_type=MESH
                )
                count += 1
    if ranks > 1:
        for side in (left, right):
            pl.semaphore_signal(barrier, inc=1, device_id=(side, head), device_id_type=MESH)
            count += 1

    own_copies = [
        pltpu.make_async_copy(w.at[pl.ds(g * each, each)], own_w.at[i], own_sem.at[i])
        for i, w in enumerate((w_one, w_three, w_two))
    ]
    value_copies = [
        pltpu.make_async_copy(values.at[s], v_buf.at[s], v_sem.at[s]) for s in range(seqs)
    ]
    for copy in value_copies:
        copy.start()
    pl.semaphore_wait(barrier, count)

    def token_parts(kind, c, peer):
        s, h = lax.div(c, each), peer * each + lax.rem(c, each)
        if kind == 0:
            source = keys.at[s, :, cols(h)]
        elif kind == 1:
            source = v_buf.at[s, :, cols(h)]
        else:
            source = queries.at[s, 1, :, cols(h)]
        return source, (k_buf, s_buf, q_buf)[kind].at[c, block(g), :]

    def token_copy(kind, c, j):
        peer = member(j)
        src, dst = token_parts(kind, c, peer)
        return pltpu.make_async_remote_copy(
            src_ref=src, dst_ref=dst,
            send_sem=tok_send.at[kind, c, j], recv_sem=tok_recv.at[kind, c, j],
            device_id=(base + peer, head), device_id_type=MESH,
        )

    def token_local(kind, c):
        src, dst = token_parts(kind, c, g)
        return pltpu.make_async_copy(src, dst, local_sem.at[kind, c])

    def scale(c, j):
        s, h = lax.div(c, each), member(j) * each + lax.rem(c, each)
        table = rates[s]
        lane = lax.broadcasted_iota(jnp.int32, table.shape, 1)
        rate = jnp.sum(jnp.where(lane == h, table, 0.0), axis=1, keepdims=True)
        v_buf[s, :, cols(h)] = (-rate * v_buf[s, :, cols(h)].astype(F32)).astype(BF16)

    for s in range(seqs):
        for e in range(each):
            c = jnp.int32(s * each + e)

            def send_keys(j, carry, c=c):
                token_copy(0, c, j).start()
                return carry

            lax.fori_loop(1, members, send_keys, 0)
            token_local(0, c).start()
            if e == 0:
                value_copies[s].wait()

            def send_scaled(j, carry, c=c):
                scale(c, j)
                token_copy(1, c, j).start()
                return carry

            lax.fori_loop(1, members, send_scaled, 0)
            scale(c, 0)
            token_local(1, c).start()
    for copy in own_copies:
        copy.start()

    def fetch(h, slot):
        copies = [
            pltpu.make_async_copy(w.at[h], w_slot.at[slot, i], slot_sem.at[slot, i])
            for i, w in enumerate((w_one, w_three, w_two))
        ]
        for s in range(seqs):
            copies.append(
                pltpu.make_async_copy(
                    queries.at[s, 0, :, cols(h)],
                    x_slot.at[slot, pl.ds(s * rows, rows), :],
                    slot_sem.at[slot, 3 + s],
                )
            )
        return copies

    def first_parts(h, s, dest):
        return (
            first_buf.at[h, pl.ds(pl.multiple_of(s * rows + dest * sub, sub), sub), :],
            out.at[s, 0, :, cols(head * heads + h)],
        )

    def first_copy(h, s, k):
        dest = peer_head(k)
        src, dst = first_parts(h, s, dest)
        return pltpu.make_async_remote_copy(
            src_ref=src, dst_ref=dst,
            send_sem=first_send.at[h, s, k], recv_sem=first_recv.at[h, s, k],
            device_id=(tok, dest), device_id_type=MESH,
        )

    def first_own(h, s):
        src, dst = first_parts(h, s, head)
        return pltpu.make_async_copy(src, dst, first_local.at[h, s])

    for copy in fetch(0, 0):
        copy.start()

    def first_body(h, carry):
        slot = lax.rem(h, 2)

        @pl.when(h + 1 < heads)
        def _():
            for copy in fetch(h + 1, lax.rem(h + 1, 2)):
                copy.start()

        for copy in fetch(h, slot):
            copy.wait()
        first_buf[h] = fast_map(x_slot[slot], w_slot[slot, 0], w_slot[slot, 1], w_slot[slot, 2])
        for s in range(seqs):
            for k in range(1, n_head):
                first_copy(h, s, k).start()
            first_own(h, s).start()
        return carry

    lax.fori_loop(0, heads, first_body, 0)
    for copy in own_copies:
        copy.wait()

    def add_block(c, b):
        e = lax.rem(c, each)
        key_rows = k_buf[c, block(b), :]
        scaled_rows = s_buf[c, block(b), :]
        gate = dot(key_rows, own_w[0, e])
        up = dot(key_rows, own_w[1, e])
        back = dot_nt(scaled_rows, own_w[2, e])
        sig = jax.nn.sigmoid(gate)
        swish = gate * sig
        hidden = (swish * up).astype(BF16)
        d_up = (back * swish).astype(BF16)
        d_gate = (back * up * sig * (1.0 + gate * (1.0 - sig))).astype(BF16)
        acc[0] += dot_tn(key_rows, d_gate)
        acc[1] += dot_tn(key_rows, d_up)
        acc[2] += dot_tn(hidden, scaled_rows)

    def gradients(c):
        acc[...] = jnp.zeros_like(acc)
        for kind in (0, 1):
            token_local(kind, c).wait()
        add_block(c, g)

        def body(j, carry):
            for kind in (0, 1):
                token_copy(kind, c, j).wait_recv()
            add_block(c, lax.rem(g + members - j, members))
            return carry

        lax.fori_loop(1, members, body, 0)
        for i in range(3):
            own[3 * c + i] = acc[i].astype(BF16)

        def send_queries(j, carry):
            token_copy(2, c, j).start()
            return carry

        lax.fori_loop(1, members, send_queries, 0)
        token_local(2, c).start()

    def right_copy(u):
        return pltpu.make_async_remote_copy(
            src_ref=from_left.at[u], dst_ref=from_left.at[u],
            send_sem=right_send.at[u], recv_sem=right_recv.at[u],
            device_id=(right, head), device_id_type=MESH,
        )

    def left_copy(u):
        return pltpu.make_async_remote_copy(
            src_ref=from_right.at[u], dst_ref=from_right.at[u],
            send_sem=left_send.at[u], recv_sem=left_recv.at[u],
            device_id=(left, head), device_id_type=MESH,
        )

    def pass_on(u, place, sums, copy):
        @pl.when(jnp.logical_and(u >= 0, u < units))
        def _():
            @pl.when(place == 0)
            def _():
                sums[u] = own[u]

            if ranks > 1:
                @pl.when(place > 0)
                def _():
                    copy(u).wait_recv()
                    sums[u] = (sums[u].astype(F32) + own[u].astype(F32)).astype(BF16)

                @pl.when(place < ranks - 1)
                def _():
                    copy(u).start()

    def second_parts(c, b, dest):
        h = head * heads + g * each + lax.rem(c, each)
        return (
            q_buf.at[c, pl.ds(pl.multiple_of(b * rows + dest * sub, sub), sub), :],
            out.at[lax.div(c, each), 1, :, cols(h)],
        )

    def second_copy(c, j, k):
        b, dest = member(j), peer_head(k)
        src, dst = second_parts(c, b, dest)
        return pltpu.make_async_remote_copy(
            src_ref=src, dst_ref=dst,
            send_sem=second_send.at[c, j, k], recv_sem=second_recv.at[c, j, k],
            device_id=(base + b, dest), device_id_type=MESH,
        )

    def second_own(c):
        src, dst = second_parts(c, g, head)
        return pltpu.make_async_copy(src, dst, second_local.at[c])

    def second(c):
        def map_block(b):
            q_buf[c, block(b), :] = fast_map(
                q_buf[c, block(b), :], renewed[0], renewed[1], renewed[2]
            )

        def body(j, carry):
            token_copy(2, c, j).wait_recv()
            b = lax.rem(g + members - j, members)
            map_block(b)
            for k in range(n_head):
                second_copy(c, lax.rem(members - j, members), k).start()
            return carry

        lax.fori_loop(1, members, body, 0)
        token_local(2, c).wait()
        map_block(g)
        for k in range(1, n_head):
            second_copy(c, 0, k).start()
        second_own(c).start()

    def renew(u):
        c, i = lax.div(u, 3), lax.rem(u, 3)
        e = lax.rem(c, each)
        total = from_left[u].astype(F32) + from_right[u].astype(F32) - own[u].astype(F32)
        mean_sq = jnp.mean(
            jnp.mean(total * total, axis=0, keepdims=True), axis=1, keepdims=True
        )
        factor = step_size[g * each + e] * lax.rsqrt(mean_sq + 1e-05)
        renewed[i] = (own_w[i, e].astype(F32) - factor * total).astype(BF16)

    def slot_body(t, carry):
        @pl.when(jnp.logical_and(lax.rem(t, 3) == 0, t < units))
        def _():
            gradients(lax.div(t, 3))

        pass_on(t - rank, rank, from_left, right_copy)
        pass_on(t - (ranks - 1 - rank), ranks - 1 - rank, from_right, left_copy)
        u = t - (ranks - 1)

        @pl.when(u >= 0)
        def _():
            renew(u)

            @pl.when(lax.rem(u, 3) == 2)
            def _():
                second(lax.div(u, 3))

        return carry

    lax.fori_loop(0, units + ranks - 1, slot_body, 0)

    def drain_first(h, carry):
        for s in range(seqs):
            for k in range(1, n_head):
                first_copy(h, s, k).wait()
            first_own(h, s).wait()
        return carry

    lax.fori_loop(0, heads, drain_first, 0)

    def drain_chunk(c, carry):
        for k in range(1, n_head):
            second_copy(c, 0, k).wait()
        second_own(c).wait()

        def drain_member(j, inner):
            for kind in range(3):
                token_copy(kind, c, j).wait_send()
            for k in range(n_head):
                second_copy(c, j, k).wait()
            return inner

        lax.fori_loop(1, members, drain_member, 0)
        return carry

    lax.fori_loop(0, chunks, drain_chunk, 0)

    if ranks > 1:
        def drain_sums(u, carry):
            @pl.when(rank < ranks - 1)
            def _():
                right_copy(u).wait_send()

            @pl.when(rank > 0)
            def _():
                left_copy(u).wait_send()

            return carry

        lax.fori_loop(0, units, drain_sums, 0)


def norm_kernel(block_rows, gain, normed):
    values = block_rows[...].astype(F32)
    mean_sq = jnp.mean(values * values, axis=-1, keepdims=True)
    normed[...] = (values * lax.rsqrt(mean_sq + 1e-06) * gain[...]).astype(BF16)


def solution(mesh):
    n_tok, n_head = mesh.shape["tok"], mesh.shape["head"]

    def shards(
        queries, first_keys, first_values, first_rates, w_one, w_three, w_two, step_size, out_gain
    ):
        seqs, groups, rows, here = queries.shape
        heads, hd, hh = w_one.shape
        members = math.gcd(4, heads, n_tok)
        each = heads // members
        chunks = seqs * each
        units = 3 * chunks
        sub = rows // n_head
        width = here * n_head
        rates = jnp.transpose(first_rates, (0, 2, 1))
        anywhere = pl.BlockSpec(memory_space=pl.ANY)
        vmem = pl.BlockSpec(memory_space=pltpu.VMEM)
        smem = pl.BlockSpec(memory_space=pltpu.SMEM)
        sem = pltpu.SemaphoreType.DMA
        dims = (n_tok, n_head, seqs, heads, rows, hd, members)
        tokens = (chunks, members * rows, hd)
        flops = 24 * seqs * heads * rows * hd * hh
        merged = pl.pallas_call(
            functools.partial(kernel, dims),
            out_shape=jax.ShapeDtypeStruct((seqs, groups, sub, width), BF16),
            in_specs=[anywhere] * 6 + [smem, vmem],
            out_specs=anywhere,
            scratch_shapes=[
                pltpu.VMEM(tokens, BF16),
                pltpu.VMEM(tokens, BF16),
                pltpu.VMEM(tokens, BF16),
                pltpu.VMEM((seqs, rows, here), BF16),
                pltpu.VMEM((2, 3, hd, hh), BF16),
                pltpu.VMEM((2, seqs * rows, hd), BF16),
                pltpu.VMEM((3, each, hd, hh), BF16),
                pltpu.VMEM((heads, seqs * rows, hd), BF16),
                pltpu.VMEM((3, hd, hh), F32),
                pltpu.VMEM((units, hd, hh), BF16),
                pltpu.VMEM((units, hd, hh), BF16),
                pltpu.VMEM((units, hd, hh), BF16),
                pltpu.VMEM((3, hd, hh), BF16),
                sem((2, 3 + seqs)),
                sem((3,)),
                sem((seqs,)),
                sem((3, chunks)),
                sem((3, chunks, members)),
                sem((3, chunks, members)),
                sem((heads, seqs, n_head)),
                sem((heads, seqs, n_head)),
                sem((heads, seqs)),
                sem((units,)),
                sem((units,)),
                sem((units,)),
                sem((units,)),
                sem((chunks, members, n_head)),
                sem((chunks, members, n_head)),
                sem((chunks,)),
            ],
            compiler_params=pltpu.CompilerParams(
                collective_id=0, has_side_effects=True, vmem_limit_bytes=60 * 1024 * 1024
            ),
            cost_estimate=pl.CostEstimate(
                flops=flops, bytes_accessed=queries.size * 8, transcendentals=0
            ),
        )(queries, first_keys, first_values, w_one, w_three, w_two, step_size, rates)
        all_rows = seqs * groups * sub
        tile = math.gcd(64, all_rows)
        normed = pl.pallas_call(
            norm_kernel,
            grid=(all_rows // tile,),
            out_shape=jax.ShapeDtypeStruct((all_rows, width), BF16),
            in_specs=[
                pl.BlockSpec((tile, width), lambda i: (i, 0)),
                pl.BlockSpec((1, width), lambda i: (0, 0)),
            ],
            out_specs=pl.BlockSpec((tile, width), lambda i: (i, 0)),
            compiler_params=pltpu.CompilerParams(vmem_limit_bytes=32 * 1024 * 1024),
        )(merged.reshape(all_rows, width), out_gain[None, :])
        return normed.reshape(merged.shape)

    return jax.shard_map(
        shards,
        mesh=mesh,
        in_specs=(
            P(None, None, "tok", "head"),
            P(None, "tok", "head"),
            P(None, "tok", "head"),
            P(None, "head", "tok"),
            P("head", None, None),
            P("head", None, None),
            P("head", None, None),
            P("head"),
            P(),
        ),
        out_specs=P(None, None, ("tok", "head"), None),
        check_vma=False,
    )
```

time: 293 us -> 235 us (0.80)
  Pallas kernels: 262 us -> 230 us
  local copies, waits for them, and re-layouts: 21 us -> 4.93 us
  other arithmetic: 8.72 us -> 0 us
    pallas_call x1, Pallas kernels: 262 us -> 223 us  [shards(): pl.pallas_call(functools.partial(kernel, dims), out_shape=jax.ShapeDtypeS...]
    mul x2 -> x0, local copies, waits for them, and re-layouts: 13.1 us -> none  [shards(): scaled = (-rates * values).astype(BF16).reshape(first_values.shape)]
    convert_element_type x1 -> x0, other arithmetic: 8 us -> none  [shards(): scaled = (-rates * values).astype(BF16).reshape(first_values.shape)]
    pallas_call x0 -> x1, Pallas kernels: none -> 7.06 us  [shards(): pl.pallas_call(norm_kernel, grid=(all_rows // tile,), out_shape=jax.Shape...]
    unnamed x1 -> x5, local copies, waits for them, and re-layouts: 7.77 us -> 4.93 us
where the time goes in v2:
time: 235 us
  Pallas kernels  230 us (98%)
  local copies, waits for them, and re-layouts  4.93 us (2%)
    pallas_call x1, Pallas kernels, shards(): pl.pallas_call(functools.partial(kernel, dims), out_shape=jax.ShapeDtypeS...  223 us
    pallas_call x1, Pallas kernels, shards(): pl.pallas_call(norm_kernel, grid=(all_rows // tile,), out_shape=jax.Shape...  7.06 us
    unnamed x5, local copies, waits for them, and re-layouts  4.93 us

profile of v2, /device:TPU:0, one launch (start us, length us, event | category | flops | bytes accessed | tf_op | source)
XLA Modules:
  0.0 234.7 jit_solution(9226235900853467223)
XLA Ops:
  0.0 1.6 copy.10
  1.6 0.0 copy-start.1
  1.6 222.7 %shard_map.91 = bf16[2,2,128,8192]{3,2,1,0:T(8,128)(2,1)} custom-call(bf16[2,2,256,4096]{3,2,1,0:T(8,128)(2,1)} %queries.1, bf16[2,256,4096]{2,1,0:T(8,128)(2,1)} %keys.1, bf16[2,256,4096]{2,1,0:T(8,128)(2,1)} %values.1, bf16[8,512,512]{2,1,0:T(8,128)(2,1)} %w_one.1, bf16[8,512,512]{2,1,0:T(8,128)(2,1)} %w_three.1, bf16[8,512,512]{2,1,0:T(8,128)(2,1)} %w_two.1, ...), custom_call_target="tpu_custom_call" | custom-call | flops 25769803776 | bytes 33554432 | tf_op jit(solution)/shard_map/pallas_call | solution.py:417
  224.2 0.0 copy-done.1
  224.2 0.0 copy-start
  224.3 3.4 %copy-done = bf16[2,2,128,8192]{3,2,1,0:T(8,128)(2,1)S(1)} copy-done((bf16[2,2,128,8192]{3,2,1,0:T(8,128)(2,1)S(1)}, bf16[2,2,128,8192]{3,2,1,0:T(8,128)(2,1)}, u32[]{:S(2)}) %copy-start) | copy-done | bytes 8388632
  227.6 7.1 %shard_map.92 = bf16[512,8192]{1,0:T(8,128)(2,1)} custom-call(bf16[512,8192]{1,0:T(8,128)(2,1)S(1)} %bitcast.4, f32[1,8192]{1,0:T(1,128)S(1)} %bitcast.5), custom_call_target="tpu_custom_call" | custom-call | tf_op jit(solution)/shard_map/pallas_call | solution.py:462
Async XLA Ops:
  1.6 222.7 %copy-start.1 = (f32[8192]{0:T(1024)S(1)}, f32[8192]{0:T(1024)}, u32[]{:S(2)}) copy-start(f32[8192]{0:T(1024)} %param.17) | copy-start | bytes 98308
  224.2 3.4 %copy-start = (bf16[2,2,128,8192]{3,2,1,0:T(8,128)(2,1)S(1)}, bf16[2,2,128,8192]{3,2,1,0:T(8,128)(2,1)}, u32[]{:S(2)}) copy-start(bf16[2,2,128,8192]{3,2,1,0:T(8,128)(2,1)} %shard_map.91) | copy-start | bytes 25165828

commit v3 on v2

--- a/solution.py
+++ b/solution.py
@@ -11,6 +11,8 @@
 MESH = pl.DeviceIdType.MESH
 F32 = jnp.float32
 BF16 = jnp.bfloat16
+PIECES = 4
+SKEW = 4
 
 
 def dot(left, right):
@@ -44,7 +46,8 @@
     n_tok, n_head, seqs, heads, rows, hd, members = dims
     each = heads // members
     chunks = seqs * each
-    units = 3 * chunks
+    span = 3 * PIECES
+    units = span * chunks
     ranks = n_tok // members
     sub = rows // n_head
     tok, head = lax.axis_index("tok"), lax.axis_index("head")
@@ -121,27 +124,31 @@
         rate = jnp.sum(jnp.where(lane == h, table, 0.0), axis=1, keepdims=True)
         v_buf[s, :, cols(h)] = (-rate * v_buf[s, :, cols(h)].astype(F32)).astype(BF16)
 
+    def start_tokens(kind, c):
+        def body(j, carry):
+            token_copy(kind, c, j).start()
+            return carry
+
+        lax.fori_loop(1, members, body, 0)
+        token_local(kind, c).start()
+
+    ahead = min(2, chunks)
     for s in range(seqs):
         for e in range(each):
             c = jnp.int32(s * each + e)
-
-            def send_keys(j, carry, c=c):
-                token_copy(0, c, j).start()
-                return carry
-
-            lax.fori_loop(1, members, send_keys, 0)
-            token_local(0, c).start()
+            early = s * each + e < ahead
+            if early:
+                start_tokens(0, c)
             if e == 0:
                 value_copies[s].wait()
 
-            def send_scaled(j, carry, c=c):
+            def scale_all(j, carry, c=c):
                 scale(c, j)
-                token_copy(1, c, j).start()
                 return carry
 
-            lax.fori_loop(1, members, send_scaled, 0)
-            scale(c, 0)
-            token_local(1, c).start()
+            lax.fori_loop(0, members, scale_all, 0)
+            if early:
+                start_tokens(1, c)
     for copy in own_copies:
         copy.start()
 
@@ -199,7 +206,8 @@
             first_own(h, s).start()
         return carry
 
-    lax.fori_loop(0, heads, first_body, 0)
+    upfront = (heads + 1) // 2
+    lax.fori_loop(0, upfront, first_body, 0)
     for copy in own_copies:
         copy.wait()
 
@@ -233,14 +241,16 @@
 
         lax.fori_loop(1, members, body, 0)
         for i in range(3):
-            own[3 * c + i] = acc[i].astype(BF16)
-
-        def send_queries(j, carry):
-            token_copy(2, c, j).start()
-            return carry
-
-        lax.fori_loop(1, members, send_queries, 0)
-        token_local(2, c).start()
+            own[pl.ds((3 * c + i) * PIECES, PIECES)] = (
+                acc[i].astype(BF16).reshape(PIECES, hd // PIECES, acc.shape[-1])
+            )
+
+        @pl.when(c + ahead < chunks)
+        def _():
+            for kind in (0, 1):
+                start_tokens(kind, c + ahead)
+
+        start_tokens(2, c)
 
     def right_copy(u):
         return pltpu.make_async_remote_copy(
@@ -314,36 +324,50 @@
             second_copy(c, 0, k).start()
         second_own(c).start()
 
-    def renew(u):
-        c, i = lax.div(u, 3), lax.rem(u, 3)
+    def renew(matrix):
+        c, i = lax.div(matrix, 3), lax.rem(matrix, 3)
         e = lax.rem(c, each)
-        total = from_left[u].astype(F32) + from_right[u].astype(F32) - own[u].astype(F32)
+        parts = pl.ds(matrix * PIECES, PIECES)
+        total = (
+            from_left[parts].astype(F32) + from_right[parts].astype(F32) - own[parts].astype(F32)
+        ).reshape(acc.shape[1:])
         mean_sq = jnp.mean(
             jnp.mean(total * total, axis=0, keepdims=True), axis=1, keepdims=True
         )
         factor = step_size[g * each + e] * lax.rsqrt(mean_sq + 1e-05)
         renewed[i] = (own_w[i, e].astype(F32) - factor * total).astype(BF16)
 
+    gradients(jnp.int32(0))
+    lead = 4
+
     def slot_body(t, carry):
-        @pl.when(jnp.logical_and(lax.rem(t, 3) == 0, t < units))
+        pass_on(t - SKEW * rank, rank, from_left, right_copy)
+        pass_on(t - SKEW * (ranks - 1 - rank), ranks - 1 - rank, from_right, left_copy)
+        u = t - SKEW * (ranks - 1)
+
+        @pl.when(jnp.logical_and(u >= 0, lax.rem(u, PIECES) == PIECES - 1))
         def _():
-            gradients(lax.div(t, 3))
-
-        pass_on(t - rank, rank, from_left, right_copy)
-        pass_on(t - (ranks - 1 - rank), ranks - 1 - rank, from_right, left_copy)
-        u = t - (ranks - 1)
-
-        @pl.when(u >= 0)
+            renew(lax.div(u, PIECES))
+
+            @pl.when(lax.rem(u, span) == span - 1)
+            def _():
+                second(lax.div(u, span))
+
+        h = upfront + lax.div(t, 2)
+
+        @pl.when(jnp.logical_and(lax.rem(t, 2) == 0, h < heads))
         def _():
-            renew(u)
-
-            @pl.when(lax.rem(u, 3) == 2)
-            def _():
-                second(lax.div(u, 3))
+            first_body(h, 0)
+
+        later = t + lead
+
+        @pl.when(jnp.logical_and(lax.rem(later, span) == 0, later < units))
+        def _():
+            gradients(lax.div(later, span))
 
         return carry
 
-    lax.fori_loop(0, units + ranks - 1, slot_body, 0)
+    lax.fori_loop(0, units + SKEW * (ranks - 1), slot_body, 0)
 
     def drain_first(h, carry):
         for s in range(seqs):
@@ -403,7 +427,7 @@
         members = math.gcd(4, heads, n_tok)
         each = heads // members
         chunks = seqs * each
-        units = 3 * chunks
+        units = 3 * PIECES * chunks
         sub = rows // n_head
         width = here * n_head
         rates = jnp.transpose(first_rates, (0, 2, 1))
@@ -429,9 +453,9 @@
                 pltpu.VMEM((3, each, hd, hh), BF16),
                 pltpu.VMEM((heads, seqs * rows, hd), BF16),
                 pltpu.VMEM((3, hd, hh), F32),
-                pltpu.VMEM((units, hd, hh), BF16),
-                pltpu.VMEM((units, hd, hh), BF16),
-                pltpu.VMEM((units, hd, hh), BF16),
+                pltpu.VMEM((units, hd // PIECES, hh), BF16),
+                pltpu.VMEM((units, hd // PIECES, hh), BF16),
+                pltpu.VMEM((units, hd // PIECES, hh), BF16),
                 pltpu.VMEM((3, hd, hh), BF16),
                 sem((2, 3 + seqs)),
                 sem((3,)),
@@ -468,7 +492,7 @@
                 pl.BlockSpec((1, width), lambda i: (0, 0)),
             ],
             out_specs=pl.BlockSpec((tile, width), lambda i: (i, 0)),
-            compiler_params=pltpu.CompilerParams(vmem_limit_bytes=32 * 1024 * 1024),
+            compiler_params=pltpu.CompilerParams(vmem_limit_bytes=60 * 1024 * 1024),
         )(merged.reshape(all_rows, width), out_gain[None, :])
         return normed.reshape(merged.shape)
 

time: 235 us -> 217 us (0.923)
  Pallas kernels: 230 us -> 215 us
  local copies, waits for them, and re-layouts: 4.93 us -> 1.55 us
    pallas_call x1, Pallas kernels: 223 us -> 204 us  [shards(): pl.pallas_call(functools.partial(kernel, dims), out_shape=jax.ShapeDtypeS...]
    pallas_call x1, Pallas kernels: 7.06 us -> 10.5 us  [shards(): pl.pallas_call(norm_kernel, grid=(all_rows // tile,), out_shape=jax.Shape...]
    unnamed x5 -> x1, local copies, waits for them, and re-layouts: 4.93 us -> 1.55 us
where the time goes in v3:
time: 217 us; the launch traced here: 216 us
  Pallas kernels  215 us (99%)
    pallas_call x1, Pallas kernels, shards(): pl.pallas_call(functools.partial(kernel, dims), out_shape=jax.ShapeDtypeS...  204 us
    pallas_call x1, Pallas kernels, shards(): pl.pallas_call(norm_kernel, grid=(all_rows // tile,), out_shape=jax.Shape...  10.5 us

profile of v3, /device:TPU:0, one launch (start us, length us, event | category | flops | bytes accessed | tf_op | source)
XLA Modules:
  0.0 216.1 jit_solution(670772535979398245)
XLA Ops:
  0.0 1.6 copy.10
  1.6 204.1 %shard_map.91 = bf16[2,2,128,8192]{3,2,1,0:T(8,128)(2,1)} custom-call(bf16[2,2,256,4096]{3,2,1,0:T(8,128)(2,1)} %queries.1, bf16[2,256,4096]{2,1,0:T(8,128)(2,1)} %keys.1, bf16[2,256,4096]{2,1,0:T(8,128)(2,1)} %values.1, bf16[8,512,512]{2,1,0:T(8,128)(2,1)} %w_one.1, bf16[8,512,512]{2,1,0:T(8,128)(2,1)} %w_three.1, bf16[8,512,512]{2,1,0:T(8,128)(2,1)} %w_two.1, ...), custom_call_target="tpu_custom_call" | custom-call | flops 25769803776 | bytes 33554432 | tf_op jit(solution)/shard_map/pallas_call | solution.py:441
  205.6 10.5 %shard_map.92 = bf16[512,8192]{1,0:T(8,128)(2,1)} custom-call(bf16[512,8192]{1,0:T(8,128)(2,1)} %bitcast.4, f32[1,8192]{1,0:T(1,128)} %bitcast.6), custom_call_target="tpu_custom_call" | custom-call | tf_op jit(solution)/shard_map/pallas_call | solution.py:486
